TPU v7x, 128 devices: a whole 4x4x4 slice. The times are simulated.
128 devices in a mesh: section: 16 (over z, y_lo, core), tensor: 8 (over y_hi, x).
Axes of the slice: x: 4, y: 4 (y_hi: 2, y_lo: 2; y = y_hi * 2 + y_lo), z: 4, core: 2. Of those that a mesh axis runs over, the one named last changes fastest.
Arguments:
- token_ids: int32 [4096], P('section'), may hold values from 0 to 152063, as said below
- column_order: int32 [8192], replicated, may hold values from 0 to 8191, each once
- residual: bfloat16 [4096, 8192], P('section', 'tensor'), may hold values from -40 to 40
- attn_out: bfloat16 [4096, 8192], P('section', 'tensor'), may hold values from -6 to 6
- out_proj: bfloat16 [8192, 8192], P(None, 'tensor'), may hold values from -0.0625 to 0.0625
- norm_gain: float32 [8192], P('tensor'), may hold values from 0.5 to 1.5
Outputs:
- factored: float32 [8192, 8192], P('section', 'tensor')
Inputs may be any that keep to these rules, and one draw needn't show every extreme that they name: `token_ids`: id 0 marks padding. In each block of 256 tokens of one section index the padding fills trailing positions, and each block holds at least one non-padding token.
All inputs are finite; a program needn't handle non-finite values.
Results may differ from a plain program's by a relative error of at most 0.0067.
Values may be sent and summed in bfloat16 or wider, within the bound.
No kernel may reach another device: no remote copies, remote signals or barrier semaphores. Data moves between devices by JAX's collectives and lax.ppermute only.
A program may use at most 128 MiB of HBM per device.

v0:
```python
import jax
import jax.numpy as jnp
from jax import lax
from jax.sharding import PartitionSpec as P

TILE = 128
PANEL = 1024
epsilon = 1e-06


def spread(value, axis, source):
    kept = jnp.where(lax.axis_index(axis) == source, value, 0).astype(value.dtype)
    return lax.psum(kept, axis)


def shards(token_ids, column_order, residual, attn_out, out_proj, norm_gain):
    section_count = lax.axis_size("section")
    tensor_count = lax.axis_size("tensor")
    section_id = lax.axis_index("section")
    tensor_id = lax.axis_index("tensor")
    model_width = out_proj.shape[0]
    span_rows = model_width // section_count
    span_cols = model_width // tensor_count
    projected = jnp.dot(
        lax.all_gather(attn_out, "tensor", axis=1, tiled=True),
        out_proj,
        preferred_element_type=jnp.float32,
    )
    rounded = (residual.astype(jnp.float32) + projected).astype(jnp.bfloat16)
    hidden = lax.optimization_barrier(rounded).astype(jnp.float32)
    squares = lax.psum(jnp.sum(hidden * hidden, axis=1), "tensor")
    kept_rows = (token_ids != 0).astype(jnp.float32)
    token_count = lax.psum(jnp.sum(kept_rows), "section")
    row_scale = lax.rsqrt(squares / model_width + epsilon) * kept_rows
    normed = (hidden * row_scale[:, None] * norm_gain[None, :]).astype(jnp.bfloat16)
    target = jnp.arange(section_count, dtype=jnp.int32)[:, None, None]
    tile_index = jnp.arange(span_rows // TILE, dtype=jnp.int32)[None, :, None]
    offset = jnp.arange(TILE, dtype=jnp.int32)[None, None, :]
    send_global = ((tile_index * section_count + target) * TILE + offset).reshape(model_width)
    col_tiles = jnp.arange(span_cols // TILE, dtype=jnp.int32)[:, None]
    cols_global = (
        (col_tiles * tensor_count + tensor_id) * TILE + jnp.arange(TILE, dtype=jnp.int32)[None, :]
    ).reshape(span_cols)
    full_rows = lax.all_gather(normed, "tensor", axis=1, tiled=True)
    outgoing = jnp.take(full_rows, jnp.take(column_order, send_global), axis=1)
    mine_rows = lax.all_to_all(outgoing, "section", split_axis=1, concat_axis=0, tiled=True)
    col_part = jnp.take(full_rows, jnp.take(column_order, cols_global), axis=1)
    gram_sum = lax.dot_general(
        mine_rows,
        lax.all_gather(col_part, "section", axis=0, tiled=True),
        (((0,), (0,)), ((), ())),
        preferred_element_type=jnp.float32,
    )
    hessian = gram_sum / token_count
    panel_local = PANEL // tensor_count
    per_group = panel_local // TILE
    gathered = lax.all_gather(hessian[:, :panel_local], "tensor", axis=1, tiled=True)
    panel_rows = (
        gathered.reshape(span_rows, tensor_count, per_group, TILE)
        .transpose(0, 2, 1, 3)
        .reshape(span_rows, PANEL)
    )
    first_tile = panel_rows[:TILE]
    stacked = lax.all_gather(first_tile, "section", axis=0, tiled=True)
    diag_block = stacked[:PANEL]
    chol_low = jnp.linalg.cholesky(diag_block)
    own_lower = lax.linalg.triangular_solve(
        chol_low, panel_rows, left_side=False, lower=True, transpose_a=True
    )
    copies = [
        spread(own_lower, "section", tensor_id + second * tensor_count)
        for second in range(section_count // tensor_count)
    ]
    shaped = [copy_rows.reshape(span_rows // TILE, TILE, PANEL) for copy_rows in copies]
    other_lower = jnp.stack(shaped, axis=1).reshape(span_cols, PANEL)
    row_tiles = jnp.arange(span_rows // TILE, dtype=jnp.int32)[:, None]
    rows_global = (
        (row_tiles * section_count + section_id) * TILE + jnp.arange(TILE, dtype=jnp.int32)[None, :]
    ).reshape(span_rows)
    panel_global = cols_global[:panel_local]
    left_part = jnp.take(own_lower, panel_global, axis=1)
    left_part = jnp.where(
        rows_global[:, None] >= panel_global[None, :], left_part, jnp.float32(0.0)
    )
    update = jnp.dot(
        own_lower,
        other_lower[panel_local:].T,
        precision=lax.Precision.HIGHEST,
        preferred_element_type=jnp.float32,
    )
    right_part = hessian[:, panel_local:] - update
    return jnp.concatenate([left_part, right_part], axis=1)


def solution(mesh):
    placed = (
        P("section"),
        P(),
        P("section", "tensor"),
        P("section", "tensor"),
        P(None, "tensor"),
        P("tensor"),
    )
    return jax.shard_map(
        shards, mesh=mesh, in_specs=placed, out_specs=P("section", "tensor"), check_vma=False
    )
```

profile of v0, /device:TPU:0, one launch (start us, length us, event | category | flops | bytes accessed | tf_op | source)
XLA Modules:
  0.0 999.8 jit_solution(9918803187925176559)
XLA Ops:
  7.3 76.3 %all-gather.6.cloned.1.call-done = bf16[256,8192]{1,0:T(8,128)(2,1)} async-done(((bf16[256,1024]{1,0:T(8,128)(2,1)}), bf16[256,8192]{1,0:T(8,128)(2,1)}) %all-gather.6.cloned.1.call-update) | async-done | bytes 4194320 | tf_op jit(solution)/shard_map/all_gather | solution.py:25
  83.7 11.5 %fusion.5 = bf16[256,1024]{1,0:T(8,128)(2,1)S(1)} fusion(bf16[256,8192]{1,0:T(8,128)(2,1)} %all-gather.6.cloned.1.call-done, bf16[8192,1024]{1,0:T(8,128)(2,1)} %param.10, bf16[256,1024]{1,0:T(8,128)(2,1)} %param.8), kind=kOutput, calls=%fused_computation.21 | convolution fusion | flops 4295753728 | bytes 22020096 | tf_op jit(solution)/shard_map/dot_general | solution.py:24
  95.3 19.8 %psum.28 = f32[256]{0:T(256)S(1)} all-reduce(f32[256]{0:T(256)S(1)} %fusion.6), channel_id=1, replica_groups=mesh['section'=16,'tensor'=8] {'tensor'}, use_global_device_ids=true, to_apply=%region_1.0 | all-reduce | flops 256 | bytes 2048 | tf_op jit(solution)/shard_map/psum | solution.py:31
  117.0 6.2 gather_fusion.2
  123.2 64.0 %all-gather.8.cloned.1.call-done = bf16[256,8192]{1,0:T(8,128)(2,1)} async-done(((bf16[256,1024]{1,0:T(8,128)(2,1)}), bf16[256,8192]{1,0:T(8,128)(2,1)}) %all-gather.8.cloned.1.call-update) | async-done | bytes 4194320 | tf_op jit(solution)/shard_map/all_gather | solution.py:44
  187.3 6.4 copy.13
  193.6 6.2 gather_fusion.3
  201.0 45.5 %gather_fusion = s32[8192]{0:T(1024)S(1)} fusion(s32[8192]{0:T(1024)S(1)} %copy-done, s32[8192]{0:T(1024)S(1)} %broadcast_clamp_fusion.1), kind=kCustom, calls=%fused_computation | custom fusion | bytes 98304 | tf_op jit(solution)/shard_map/jit(_take)/gather | solution.py:45
  246.7 33.9 %gather_fusion.1 = bf16[8192,256]{1,0:T(8,128)(2,1)} fusion(bf16[256,8192]{0,1:T(8,128)(2,1)} %copy.13, s32[8192]{0:T(1024)S(1)} %broadcast_clamp_fusion), kind=kCustom, calls=%fused_computation.1 | custom fusion | bytes 8421376 | tf_op jit(solution)/shard_map/jit(_take)/gather | solution.py:45
  280.6 6.4 copy.14
  287.0 4.6 broadcast_select_fusion
  291.6 4.6 all-to-all-start
  296.2 72.6 %psum.29 = f32[]{:T(128)} all-reduce(f32[]{:T(128)} %get-tuple-element.74), channel_id=1, replica_groups=mesh['section'=16,'tensor'=8] {'section'}, use_global_device_ids=true, to_apply=%region_3.0 | all-reduce | flops 1 | bytes 8 | tf_op jit(solution)/shard_map/psum | solution.py:33
  368.9 8.8 convolution_divide_fusion
  379.8 51.4 %all-gather.12.cloned.1.call-done = f32[512,1024]{0,1:T(8,128)} async-done(((f32[512,128]{0,1:T(8,128)}), f32[512,1024]{0,1:T(8,128)}) %all-gather.12.cloned.1.call-update) | async-done | bytes 2097168 | tf_op jit(solution)/shard_map/all_gather | solution.py:57
  431.3 1.9 slice.273
  433.3 59.7 %all-gather.14.cloned.1.call-done = f32[2048,1024]{0,1:T(8,128)} async-done(((f32[128,1024]{0,1:T(8,128)}), f32[2048,1024]{0,1:T(8,128)}) %all-gather.14.cloned.1.call-update) | async-done | bytes 8388624 | tf_op jit(solution)/shard_map/all_gather | solution.py:64
  493.0 4.7 slice.274
  497.8 5.5 copy.17
  503.2 4.4 fusion
  507.7 2.0 copy-done.2
  509.7 11.7 %cholesky.223 = f32[128,128]{1,0:T(8,128)S(1)} custom-call(f32[128,128]{1,0:T(8,128)S(1)} %cholesky.580), custom_call_target="Cholesky" | custom-call | tf_op jit(solution)/shard_map/jit(cholesky)/cholesky | solution.py:66
  521.5 9.8 custom-call.62
  531.3 2.6 cholesky.255
  533.8 2.4 constant_dynamic-update-slice_fusion.32
  537.8 11.9 %cholesky.244 = f32[128,128]{1,0:T(8,128)S(1)} custom-call(f32[128,128]{1,0:T(8,128)S(1)} %cholesky.584), custom_call_target="Cholesky" | custom-call | tf_op jit(solution)/shard_map/jit(cholesky)/cholesky | solution.py:66
  550.3 9.8 custom-call.63
  561.4 2.1 convolution_subtract_fusion.1
  563.5 11.7 %cholesky.468 = f32[128,128]{1,0:T(8,128)S(1)} custom-call(f32[128,128]{1,0:T(8,128)S(1)} %cholesky.589), custom_call_target="Cholesky" | custom-call | tf_op jit(solution)/shard_map/jit(cholesky)/cholesky | solution.py:66
  576.5 9.8 custom-call.64
  587.5 2.3 convolution_subtract_fusion.2
  589.8 12.1 %cholesky.487 = f32[128,128]{1,0:T(8,128)S(1)} custom-call(f32[128,128]{1,0:T(8,128)S(1)} %cholesky.594), custom_call_target="Cholesky" | custom-call | tf_op jit(solution)/shard_map/jit(cholesky)/cholesky | solution.py:66
  603.2 9.8 custom-call.65
  614.1 2.3 convolution_subtract_fusion.10
  616.5 11.7 %cholesky.506 = f32[128,128]{1,0:T(8,128)S(1)} custom-call(f32[128,128]{1,0:T(8,128)S(1)} %cholesky.599), custom_call_target="Cholesky" | custom-call | tf_op jit(solution)/shard_map/jit(cholesky)/cholesky | solution.py:66
  629.5 9.9 custom-call.66
  640.5 2.3 convolution_subtract_fusion.11
  642.7 11.7 %cholesky.526 = f32[128,128]{1,0:T(8,128)S(1)} custom-call(f32[128,128]{1,0:T(8,128)S(1)} %cholesky.604), custom_call_target="Cholesky" | custom-call | tf_op jit(solution)/shard_map/jit(cholesky)/cholesky | solution.py:66
  655.8 9.8 custom-call.67
  666.5 2.0 convolution_subtract_fusion.12
  668.6 11.9 %cholesky.546 = f32[128,128]{1,0:T(8,128)S(1)} custom-call(f32[128,128]{1,0:T(8,128)S(1)} %cholesky.609), custom_call_target="Cholesky" | custom-call | tf_op jit(solution)/shard_map/jit(cholesky)/cholesky | solution.py:66
  681.8 9.8 custom-call.68
  692.4 1.9 convolution_subtract_fusion.13
  694.3 11.7 %cholesky.564 = f32[128,128]{1,0:T(8,128)S(1)} custom-call(f32[128,128]{1,0:T(8,128)S(1)} %convolution_subtract_fusion.13), custom_call_target="Cholesky" | custom-call | tf_op jit(solution)/shard_map/jit(cholesky)/cholesky | solution.py:66
  712.9 4.9 select_select_fusion
  717.8 22.9 %while.1 = (s32[]{:T(128)}, f32[1024,1024]{1,0:T(8,128)}, s32[8,2]{0,1:T(2,128)S(1)}, f32[8,128,128]{2,1,0:T(8,128)S(1)}, s32[]{:T(128)}) while((s32[]{:T(128)}, f32[1024,1024]{1,0:T(8,128)}, s32[8,2]{0,1:T(2,128)S(1)}, f32[8,128,128]{2,1,0:T(8,128)S(1)}, s32[]{:T(128)}) %tuple.59), condition=%wide.while_cond, body=%wide.while_body.sunk | while | flops 2 | bytes 131181 | solution.py:67
  718.5 2.2 bitcast_dynamic-update-slice_fusion.2
  721.3 2.2 bitcast_dynamic-update-slice_fusion.2
  724.2 2.2 bitcast_dynamic-update-slice_fusion.2
  727.1 2.2 bitcast_dynamic-update-slice_fusion.2
  729.9 2.2 bitcast_dynamic-update-slice_fusion.2
  732.8 2.2 bitcast_dynamic-update-slice_fusion.2
  735.7 2.2 bitcast_dynamic-update-slice_fusion.2
  738.5 2.2 bitcast_dynamic-update-slice_fusion.2
  740.7 79.0 %custom-call.69 = f32[8,128,128]{1,2,0:T(8,128)S(1)} custom-call(f32[8,128,128]{2,1,0:T(8,128)S(1)} %get-tuple-element.12), custom_call_target="InvertDiagBlocksLowerTriangular" | custom-call | tf_op jit(solution)/shard_map/triangular_solve | solution.py:67
  829.4 1.9 convolution_subtract_fusion.4
  831.8 2.0 convolution_subtract_fusion.7
  834.2 2.2 convolution_subtract_fusion.3
  836.8 2.7 broadcast_select_fusion.2
  839.5 2.9 copy.24
  842.5 3.0 copy.25
  846.5 135.4 %all-reduce.4.cloned.1.call-done = (f32[4,1,128,1024]{3,2,1,0:T(8,128)}, f32[4,1,128,1024]{3,2,1,0:T(8,128)}) async-done(((f32[4,1,128,1024]{3,2,1,0:T(8,128)}, f32[4,1,128,1024]{3,2,1,0:T(8,128)}), (f32[4,1,128,1024]{3,2,1,0:T(8,128)}, f32[4,1,128,1024]{3,2,1,0:T(8,128)})) %all-reduce.4.cloned.1.call-update) | async-done | bytes 4194320 | tf_op jit(solution)/shard_map/psum | solution.py:13
  981.9 2.7 pad_maximum_fusion
  984.8 6.0 slice_subtract_fusion
  (120 shorter events, 42.5 us)
Async XLA Ops:
  6.5 110.4 %copy-start = (s32[8192]{0:T(1024)S(1)}, s32[8192]{0:T(1024)}, u32[]{:S(2)}) copy-start(s32[8192]{0:T(1024)} %param.7) | copy-start | bytes 98308
  6.5 77.1 %all-gather.6.cloned.1.call-start = ((), (), s32[]{:S(2)}) async-start(), calls=%async_computation.1 | async-start | bytes 4718592 | tf_op jit(solution)/shard_map/all_gather | solution.py:25
  7.3 107.8 %copy-start.7 = (s32[256]{0:T(256)S(1)}, s32[256]{0:T(256)}, u32[]{:S(2)}) copy-start(s32[256]{0:T(256)} %param.6) | copy-start | bytes 3076
  7.3 108.5 %copy-start.6 = (f32[1024]{0:T(1024)S(1)}, f32[1024]{0:T(1024)}, u32[]{:S(2)}) copy-start(f32[1024]{0:T(1024)} %param.11) | copy-start | bytes 12292
  7.3 180.0 %all-gather.8.cloned.1.call-start = ((), (), s32[]{:S(2)}) async-start(), calls=%async_computation.2 | async-start | bytes 4718592 | tf_op jit(solution)/shard_map/all_gather | solution.py:44
  116.8 252.1 %all-gather.10.cloned.1.call-start = ((), (), s32[]{:S(2)}) async-start(), calls=%async_computation.3 | async-start | bytes 8912896 | tf_op jit(solution)/shard_map/all_gather | solution.py:50
  291.6 77.3 %all-to-all-start = ((bf16[256,16,512]{2,0,1:T(8,128)(2,1)}), bf16[256,16,512]{2,0,1:T(8,128)(2,1)}, u32[]{:S(2)}, u32[]{:S(2)}) async-start(bf16[256,16,512]{2,0,1:T(8,128)(2,1)} %broadcast_select_fusion), calls=%async_computation | async-start | bytes 8388608 | tf_op jit(solution)/shard_map/all_to_all | solution.py:46
  296.2 135.1 %all-gather.12.cloned.1.call-start = ((), (), s32[]{:S(2)}) async-start(), calls=%async_computation.4 | async-start | bytes 2359296 | tf_op jit(solution)/shard_map/all_gather | solution.py:57
  377.7 1.3 copy-start.3
  379.8 113.2 %all-gather.14.cloned.1.call-start = ((), (), s32[]{:S(2)}) async-start(), calls=%async_computation.5 | async-start | bytes 8912896 | tf_op jit(solution)/shard_map/all_gather | solution.py:64
  433.2 548.8 %all-reduce.4.cloned.1.call-start = ((), (), s32[]{:S(2)}) async-start(), calls=%async_computation.6 | async-start | bytes 8388608 | tf_op jit(solution)/shard_map/psum | solution.py:13
  507.7 2.0 copy-start.2
  821.1 6.1 copy-start.5
  981.9 2.9 copy-start.4
  984.8 8.0 copy-start.1
Sparse Core Ops, SparseCore 0:
  9.7 73.9 all-gather.5
  116.9 70.3 all-gather.7
  201.0 58.7 all-gather.9
  379.9 51.3 all-gather.11
  433.3 59.6 all-gather.13
  845.7 136.2 all-reduce.3
where the time goes:
time: 1010 us; the launch traced here: 1000 us
  waiting for transfers between devices  388 us (38%)
  other arithmetic  274 us (27%)
  local copies, waits for them, and re-layouts  155 us (15%)
  blocking collectives  92.4 us (9%)
  matrix products  66.5 us (7%)
  between operations  19.2 us (2%)
    another operation x30, other arithmetic, shards(): chol_low = jnp.linalg.cholesky(diag_block)  172 us
    psum x1, waiting for transfers between devices, spread(): return lax.psum(kept, axis)  135 us
    gather x4, local copies, waits for them, and re-layouts, shards(): outgoing = jnp.take(full_rows, jnp.take(column_order, send_global), axis=1)  85.8 us
    another operation x3, other arithmetic, shards(): lax.linalg.triangular_solve(chol_low, panel_rows, left_side=False, lower=...  83.9 us
    all_gather x1, waiting for transfers between devices, shards(): lax.all_gather(attn_out, 'tensor', axis=1, tiled=True)  76.3 us
    psum x1, blocking collectives, shards(): token_count = lax.psum(jnp.sum(kept_rows), 'section')  72.6 us
    all_gather x1, waiting for transfers between devices, shards(): full_rows = lax.all_gather(normed, 'tensor', axis=1, tiled=True)  64 us
    all_gather x1, waiting for transfers between devices, shards(): stacked = lax.all_gather(first_tile, 'section', axis=0, tiled=True)  59.7 us
  transfers between devices with their start and end apart: 7, of which 5 were waited for; matrix products, arithmetic and copies ran while one was open for 10% of the time, Pallas kernels for 0%

commit v1 on v0

--- a/solution.py
+++ b/solution.py
@@ -61,7 +61,9 @@
         .reshape(span_rows, PANEL)
     )
     first_tile = panel_rows[:TILE]
-    stacked = lax.all_gather(first_tile, "section", axis=0, tiled=True)
+    stacked = jnp.concatenate(
+        lax.all_to_all(jnp.stack([first_tile] * lax.axis_size("section")), "section", 0, 0), axis=0
+    )
     diag_block = stacked[:PANEL]
     chol_low = jnp.linalg.cholesky(diag_block)
     own_lower = lax.linalg.triangular_solve(

time: 1010 us -> 1070 us (1.059)
  waiting for transfers between devices: 388 us -> 424 us
  matrix products: 66.5 us -> 81.4 us
    all_to_all x0 -> x1, waiting for transfers between devices: none -> 95.2 us  [shards(): lax.all_to_all(jnp.stack([first_tile] * lax.axis_size('section')), 'secti...]
    all_gather x1 -> x0, waiting for transfers between devices: 59.7 us -> none  [shards(): stacked = lax.all_gather(first_tile, 'section', axis=0, tiled=True)]
    another operation x24 -> x25, local copies, waits for them, and re-layouts: 22.7 us -> 26.9 us
  transfers between devices with their start and end apart: 7 -> 7, of which waited for: 5 -> 5; matrix products, arithmetic and copies ran while one was open for 10% -> 9% of each run, Pallas kernels for 0% -> 0%
where the time goes in v1:
time: 1070 us; the launch traced here: 1060 us
  waiting for transfers between devices  424 us (40%)
  other arithmetic  275 us (26%)
  local copies, waits for them, and re-layouts  157 us (15%)
  blocking collectives  92.4 us (9%)
  matrix products  81.4 us (8%)
  between operations  19.1 us (2%)
    another operation x30, other arithmetic, shards(): chol_low = jnp.linalg.cholesky(diag_block)  172 us
    psum x1, waiting for transfers between devices, spread(): return lax.psum(kept, axis)  134 us
    all_to_all x1, waiting for transfers between devices, shards(): lax.all_to_all(jnp.stack([first_tile] * lax.axis_size('section')), 'secti...  95.2 us
    gather x4, local copies, waits for them, and re-layouts, shards(): outgoing = jnp.take(full_rows, jnp.take(column_order, send_global), axis=1)  85.8 us
    another operation x3, other arithmetic, shards(): lax.linalg.triangular_solve(chol_low, panel_rows, left_side=False, lower=...  83.7 us
    all_gather x1, waiting for transfers between devices, shards(): lax.all_gather(attn_out, 'tensor', axis=1, tiled=True)  76.3 us
    psum x1, blocking collectives, shards(): token_count = lax.psum(jnp.sum(kept_rows), 'section')  72.6 us
    all_gather x1, waiting for transfers between devices, shards(): full_rows = lax.all_gather(normed, 'tensor', axis=1, tiled=True)  64 us
  transfers between devices with their start and end apart: 7, of which 5 were waited for; matrix products, arithmetic and copies ran while one was open for 9% of the time, Pallas kernels for 0%

profile of v1, /device:TPU:0, one launch (start us, length us, event | category | flops | bytes accessed | tf_op | source)
XLA Modules:
  0.0 1058.3 jit_solution(16531233969611916458)
XLA Ops:
  7.3 76.3 %all-gather.5.cloned.1.call-done = bf16[256,8192]{1,0:T(8,128)(2,1)} async-done(((bf16[256,1024]{1,0:T(8,128)(2,1)}), bf16[256,8192]{1,0:T(8,128)(2,1)}) %all-gather.5.cloned.1.call-update) | async-done | bytes 4194320 | tf_op jit(solution)/shard_map/all_gather | solution.py:25
  83.7 11.5 %fusion.5 = bf16[256,1024]{1,0:T(8,128)(2,1)S(1)} fusion(bf16[256,8192]{1,0:T(8,128)(2,1)} %all-gather.5.cloned.1.call-done, bf16[8192,1024]{1,0:T(8,128)(2,1)} %param.10, bf16[256,1024]{1,0:T(8,128)(2,1)} %param.8), kind=kOutput, calls=%fused_computation.23 | convolution fusion | flops 4295753728 | bytes 22020096 | tf_op jit(solution)/shard_map/dot_general | solution.py:24
  95.3 19.8 %psum.28 = f32[256]{0:T(256)S(1)} all-reduce(f32[256]{0:T(256)S(1)} %fusion.6), channel_id=1, replica_groups=mesh['section'=16,'tensor'=8] {'tensor'}, use_global_device_ids=true, to_apply=%region_1.0 | all-reduce | flops 256 | bytes 2048 | tf_op jit(solution)/shard_map/psum | solution.py:31
  117.0 6.2 gather_fusion.2
  123.2 64.0 %all-gather.7.cloned.1.call-done = bf16[256,8192]{1,0:T(8,128)(2,1)} async-done(((bf16[256,1024]{1,0:T(8,128)(2,1)}), bf16[256,8192]{1,0:T(8,128)(2,1)}) %all-gather.7.cloned.1.call-update) | async-done | bytes 4194320 | tf_op jit(solution)/shard_map/all_gather | solution.py:44
  187.3 6.4 copy.20
  193.6 6.2 gather_fusion.3
  201.0 45.5 %gather_fusion = s32[8192]{0:T(1024)S(1)} fusion(s32[8192]{0:T(1024)S(1)} %copy-done, s32[8192]{0:T(1024)S(1)} %broadcast_clamp_fusion.1), kind=kCustom, calls=%fused_computation | custom fusion | bytes 98304 | tf_op jit(solution)/shard_map/jit(_take)/gather | solution.py:45
  246.7 33.9 %gather_fusion.1 = bf16[8192,256]{1,0:T(8,128)(2,1)} fusion(bf16[256,8192]{0,1:T(8,128)(2,1)} %copy.20, s32[8192]{0:T(1024)S(1)} %broadcast_clamp_fusion), kind=kCustom, calls=%fused_computation.1 | custom fusion | bytes 8421376 | tf_op jit(solution)/shard_map/jit(_take)/gather | solution.py:45
  280.6 6.4 copy.21
  287.0 4.6 broadcast_select_fusion
  291.6 4.6 all-to-all-start
  296.2 72.6 %psum.29 = f32[]{:T(128)} all-reduce(f32[]{:T(128)} %get-tuple-element.74), channel_id=1, replica_groups=mesh['section'=16,'tensor'=8] {'section'}, use_global_device_ids=true, to_apply=%region_3.0 | all-reduce | flops 1 | bytes 8 | tf_op jit(solution)/shard_map/psum | solution.py:33
  368.8 8.9 convolution_divide_fusion
  379.9 54.0 %all-gather.11.cloned.1.call-done = f32[512,1024]{1,0:T(8,128)} async-done(((f32[512,128]{1,0:T(8,128)}), f32[512,1024]{1,0:T(8,128)}) %all-gather.11.cloned.1.call-update) | async-done | bytes 2097168 | tf_op jit(solution)/shard_map/all_gather | solution.py:57
  435.2 4.1 stack.4
  439.4 4.7 all-to-all-start.1
  444.2 95.2 %all-to-all-done.1 = f32[16,128,1024]{1,2,0:T(8,128)} async-done(((f32[16,128,1024]{1,2,0:T(8,128)}), f32[16,128,1024]{1,2,0:T(8,128)}, u32[]{:S(2)}, u32[]{:S(2)}) %all-to-all-start.1) | async-done | bytes 8388640 | tf_op jit(solution)/shard_map/all_to_all | solution.py:65
  539.4 4.7 copy_bitcast_fusion
  544.2 5.5 copy.25
  549.7 4.1 fusion
  555.8 11.7 %cholesky.223 = f32[128,128]{1,0:T(8,128)S(1)} custom-call(f32[128,128]{1,0:T(8,128)S(1)} %cholesky.580), custom_call_target="Cholesky" | custom-call | tf_op jit(solution)/shard_map/jit(cholesky)/cholesky | solution.py:68
  567.5 9.8 custom-call.62
  577.4 2.6 cholesky.255
  579.9 2.3 constant_dynamic-update-slice_fusion.32
  583.8 11.7 %cholesky.244 = f32[128,128]{1,0:T(8,128)S(1)} custom-call(f32[128,128]{1,0:T(8,128)S(1)} %cholesky.584), custom_call_target="Cholesky" | custom-call | tf_op jit(solution)/shard_map/jit(cholesky)/cholesky | solution.py:68
  596.2 10.0 custom-call.63
  607.5 2.1 convolution_subtract_fusion.1
  609.6 11.7 %cholesky.468 = f32[128,128]{1,0:T(8,128)S(1)} custom-call(f32[128,128]{1,0:T(8,128)S(1)} %cholesky.589), custom_call_target="Cholesky" | custom-call | tf_op jit(solution)/shard_map/jit(cholesky)/cholesky | solution.py:68
  622.5 9.8 custom-call.64
  633.5 2.3 convolution_subtract_fusion.2
  635.9 12.1 %cholesky.487 = f32[128,128]{1,0:T(8,128)S(1)} custom-call(f32[128,128]{1,0:T(8,128)S(1)} %cholesky.594), custom_call_target="Cholesky" | custom-call | tf_op jit(solution)/shard_map/jit(cholesky)/cholesky | solution.py:68
  649.3 9.8 custom-call.65
  660.2 2.3 convolution_subtract_fusion.10
  662.6 11.7 %cholesky.506 = f32[128,128]{1,0:T(8,128)S(1)} custom-call(f32[128,128]{1,0:T(8,128)S(1)} %cholesky.599), custom_call_target="Cholesky" | custom-call | tf_op jit(solution)/shard_map/jit(cholesky)/cholesky | solution.py:68
  675.6 9.8 custom-call.66
  686.6 2.3 convolution_subtract_fusion.11
  688.9 11.7 %cholesky.526 = f32[128,128]{1,0:T(8,128)S(1)} custom-call(f32[128,128]{1,0:T(8,128)S(1)} %cholesky.604), custom_call_target="Cholesky" | custom-call | tf_op jit(solution)/shard_map/jit(cholesky)/cholesky | solution.py:68
  701.9 9.8 custom-call.67
  714.7 11.7 %cholesky.546 = f32[128,128]{1,0:T(8,128)S(1)} custom-call(f32[128,128]{1,0:T(8,128)S(1)} %cholesky.609), custom_call_target="Cholesky" | custom-call | tf_op jit(solution)/shard_map/jit(cholesky)/cholesky | solution.py:68
  727.7 10.1 custom-call.68
  740.5 11.7 %cholesky.564 = f32[128,128]{1,0:T(8,128)S(1)} custom-call(f32[128,128]{1,0:T(8,128)S(1)} %convolution_subtract_fusion.13), custom_call_target="Cholesky" | custom-call | tf_op jit(solution)/shard_map/jit(cholesky)/cholesky | solution.py:68
  759.2 4.9 select_select_fusion
  764.1 22.9 %while.1 = (s32[]{:T(128)}, f32[1024,1024]{1,0:T(8,128)}, s32[8,2]{0,1:T(2,128)S(1)}, f32[8,128,128]{2,1,0:T(8,128)S(1)}, s32[]{:T(128)}) while((s32[]{:T(128)}, f32[1024,1024]{1,0:T(8,128)}, s32[8,2]{0,1:T(2,128)S(1)}, f32[8,128,128]{2,1,0:T(8,128)S(1)}, s32[]{:T(128)}) %tuple.59), condition=%wide.while_cond, body=%wide.while_body.sunk | while | flops 2 | bytes 131181 | solution.py:69
  764.7 2.2 bitcast_dynamic-update-slice_fusion.2
  767.6 2.2 bitcast_dynamic-update-slice_fusion.2
  770.5 2.2 bitcast_dynamic-update-slice_fusion.2
  773.3 2.2 bitcast_dynamic-update-slice_fusion.2
  776.2 2.2 bitcast_dynamic-update-slice_fusion.2
  779.1 2.2 bitcast_dynamic-update-slice_fusion.2
  781.9 2.2 bitcast_dynamic-update-slice_fusion.2
  784.8 2.2 bitcast_dynamic-update-slice_fusion.2
  787.0 78.8 %custom-call.69 = f32[8,128,128]{1,2,0:T(8,128)S(1)} custom-call(f32[8,128,128]{2,1,0:T(8,128)S(1)} %get-tuple-element.12), custom_call_target="InvertDiagBlocksLowerTriangular" | custom-call | tf_op jit(solution)/shard_map/triangular_solve | solution.py:69
  871.9 2.5 convolution_subtract_fusion.8
  874.9 2.8 convolution_subtract_fusion.9
  878.1 3.2 convolution_subtract_fusion.4
  881.8 3.6 convolution_subtract_fusion.7
  885.8 4.1 convolution_subtract_fusion.3
  890.3 2.7 broadcast_select_fusion.2
  893.0 2.9 copy.29
  896.0 3.1 copy.30
  900.2 133.6 %all-reduce.4.cloned.1.call-done = (f32[4,1,128,1024]{3,2,1,0:T(8,128)}, f32[4,1,128,1024]{3,2,1,0:T(8,128)}) async-done(((f32[4,1,128,1024]{3,2,1,0:T(8,128)}, f32[4,1,128,1024]{3,2,1,0:T(8,128)}), (f32[4,1,128,1024]{3,2,1,0:T(8,128)}, f32[4,1,128,1024]{3,2,1,0:T(8,128)})) %all-reduce.4.cloned.1.call-update) | async-done | bytes 4194320 | tf_op jit(solution)/shard_map/psum | solution.py:13
  1033.8 2.7 pad_maximum_fusion
  1036.7 13.1 %slice_subtract_fusion = f32[512,896]{1,0:T(8,128)S(1)} fusion(f32[512,1024]{1,0:T(8,128)S(1)} %copy-done.5, f32[512,1024]{0,1:T(8,128)S(1)} %convolution_dynamic-update-slice_fusion.2, f32[1024,1024]{1,0:T(8,128)S(1)} %bitcast.155), kind=kOutput, calls=%fused_computation.18 | convolution fusion | flops 5637603328 | bytes 9437184 | tf_op jit(solution)/shard_map/dot_general | solution.py:87
  (121 shorter events, 47.0 us)
Async XLA Ops:
  6.5 110.4 %copy-start = (s32[8192]{0:T(1024)S(1)}, s32[8192]{0:T(1024)}, u32[]{:S(2)}) copy-start(s32[8192]{0:T(1024)} %param.7) | copy-start | bytes 98308
  6.5 77.1 %all-gather.5.cloned.1.call-start = ((), (), s32[]{:S(2)}) async-start(), calls=%async_computation.2 | async-start | bytes 4718592 | tf_op jit(solution)/shard_map/all_gather | solution.py:25
  7.3 107.8 %copy-start.7 = (s32[256]{0:T(256)S(1)}, s32[256]{0:T(256)}, u32[]{:S(2)}) copy-start(s32[256]{0:T(256)} %param.6) | copy-start | bytes 3076
  7.3 108.5 %copy-start.6 = (f32[1024]{0:T(1024)S(1)}, f32[1024]{0:T(1024)}, u32[]{:S(2)}) copy-start(f32[1024]{0:T(1024)} %param.11) | copy-start | bytes 12292
  7.3 180.0 %all-gather.7.cloned.1.call-start = ((), (), s32[]{:S(2)}) async-start(), calls=%async_computation.3 | async-start | bytes 4718592 | tf_op jit(solution)/shard_map/all_gather | solution.py:44
  116.8 252.1 %all-gather.9.cloned.1.call-start = ((), (), s32[]{:S(2)}) async-start(), calls=%async_computation.4 | async-start | bytes 8912896 | tf_op jit(solution)/shard_map/all_gather | solution.py:50
  291.6 77.3 %all-to-all-start = ((bf16[256,16,512]{2,0,1:T(8,128)(2,1)}), bf16[256,16,512]{2,0,1:T(8,128)(2,1)}, u32[]{:S(2)}, u32[]{:S(2)}) async-start(bf16[256,16,512]{2,0,1:T(8,128)(2,1)} %broadcast_select_fusion), calls=%async_computation | async-start | bytes 8388608 | tf_op jit(solution)/shard_map/all_to_all | solution.py:46
  296.2 137.8 %all-gather.11.cloned.1.call-start = ((), (), s32[]{:S(2)}) async-start(), calls=%async_computation.5 | async-start | bytes 2359296 | tf_op jit(solution)/shard_map/all_gather | solution.py:57
  377.8 1.3 copy-start.4
  439.4 100.1 %all-to-all-start.1 = ((f32[16,128,1024]{1,2,0:T(8,128)}), f32[16,128,1024]{1,2,0:T(8,128)}, u32[]{:S(2)}, u32[]{:S(2)}) async-start(f32[16,128,1024]{1,2,0:T(8,128)} %stack.4), calls=%async_computation.1 | async-start | bytes 16777216 | tf_op jit(solution)/shard_map/all_to_all | solution.py:65
  444.1 589.7 %all-reduce.4.cloned.1.call-start = ((), (), s32[]{:S(2)}) async-start(), calls=%async_computation.6 | async-start | bytes 8388608 | tf_op jit(solution)/shard_map/psum | solution.py:13
  553.7 2.0 copy-start.2
  867.2 7.7 copy-start.3
  1033.8 2.9 copy-start.5
  1036.7 14.7 %copy-start.1 = (s32[8192]{0:T(1024)S(1)}, s32[8192]{0:T(1024)}, u32[]{:S(2)}) copy-start(s32[8192]{0:T(1024)} %param.7) | copy-start | bytes 98308
Sparse Core Ops, SparseCore 0:
  9.7 73.9 all-gather.4
  116.9 70.3 all-gather.6
  201.0 58.7 all-gather.8
  380.0 53.8 all-gather.10
  899.2 134.5 all-reduce.3
